TPU v7x, 128 devices: a whole 4x4x4 slice. The times are simulated.
128 devices in a mesh: shot: 4 (over x_lo, core), bfly: 32 (over y, x_hi, z).
Axes of the slice: x: 4 (x_hi: 2, x_lo: 2; x = x_hi * 2 + x_lo), y: 4, z: 4, core: 2. Of those that a mesh axis runs over, the one named last changes fastest.
Arguments:
- samples: float32 [4, 128, 512, 1536], P('shot', 'bfly'), may hold values from -6 to 6
- first_maps: float32 [4, 128, 128, 512], P('shot', 'bfly'), may hold values from -0.25 to 0.25
- self_maps: float32 [7, 4, 128, 128, 128], P(None, 'shot', 'bfly'), may hold values from -0.375 to 0.375
- cross_maps: float32 [7, 4, 128, 128, 128], P(None, 'shot', 'bfly'), may hold values from -0.375 to 0.375
- evaluate: float32 [128, 512, 128], P('bfly'), may hold values from -0.5 to 0.5
Outputs:
- image: float32 [1536, 65536], P('shot', 'bfly')
All inputs are finite; a program needn't handle non-finite values.
Results may differ from a plain program's by a relative error of at most 0.00011.
Values sent between devices are 32-bit elements; how exact they have to be, the bound alone decides.
A program may use at most 128 MiB of HBM per device.

v0:
```python
import jax
import jax.numpy as jnp
from jax import lax
from jax.sharding import PartitionSpec as P


def from_partner(value, axis, distance):
    mask = 2**distance
    pairs = [(source, source ^ mask) for source in range(lax.axis_size(axis))]
    return lax.ppermute(value, axis, pairs)


def shards(samples, first_maps, self_maps, cross_maps, evaluate):
    highest = lax.Precision.HIGHEST
    coef = jnp.einsum("bkq,bqc->bkc", first_maps[0], samples[0], precision=highest)
    box_dev = coef.shape[0]
    levels = self_maps.shape[0]
    swap_levels = lax.axis_size("bfly").bit_length() - 1
    local_count = levels - swap_levels
    for level in range(levels):
        own_term = jnp.einsum("bkj,bjc->bkc", self_maps[level, 0], coef, precision=highest)
        if level < local_count:
            stride = 2**level
            shape = coef.shape
            paired = coef.reshape(box_dev // (2 * stride), 2, stride, shape[1], shape[2])
            partner = paired[:, ::-1].reshape(shape)
        else:
            partner = from_partner(coef, "bfly", level - local_count)
        coef = own_term + jnp.einsum(
            "bkj,bjc->bkc", cross_maps[level, 0], partner, precision=highest
        )
    pixels = evaluate.shape[1]
    columns_dev = coef.shape[2] // lax.axis_size("shot")
    terms = jnp.einsum("bpk,bkc->cbp", evaluate, coef, precision=highest)
    return lax.psum_scatter(
        terms.reshape(lax.axis_size("shot") * columns_dev, box_dev * pixels),
        "shot",
        scatter_dimension=0,
        tiled=True,
    )


def solution(mesh):
    in_specs = (
        P("shot", "bfly", None, None),
        P("shot", "bfly", None, None),
        P(None, "shot", "bfly", None, None),
        P(None, "shot", "bfly", None, None),
        P("bfly", None, None),
    )
    out_specs = P("shot", "bfly")
    return jax.shard_map(shards, mesh=mesh, in_specs=in_specs, out_specs=out_specs, check_vma=False)
```

profile of v0, /device:TPU:1, one launch (start us, length us, event | category | flops | bytes accessed | tf_op | source)
XLA Modules:
  0.0 559.4 jit_solution(126921830415803591)
XLA Ops:
  6.5 0.0 copy-start
  6.5 0.0 reduce-scatter.2.cloned.1.call-start
  6.5 12.0 %fusion = f32[4,128,1536]{2,1,0:T(8,128)} fusion(f32[1,4,512,1536]{3,2,1,0:T(8,128)} %param.5, f32[1,4,128,512]{3,2,1,0:T(8,128)} %param.6), kind=kOutput, calls=%fused_computation | convolution fusion | flops 4831838208 | bytes 16777216 | tf_op jit(solution)/shard_map/bkq,bqc->bkc/dot_general | solution.py:15
  18.6 0.0 copy-start.3
  18.6 3.9 rev.6
  22.4 0.0 copy-done.3
  22.5 0.0 copy-start.2
  22.5 7.2 %fusion.22 = f32[4,1536,128]{2,1,0:T(8,128)S(1)} fusion(f32[4,128,1536]{2,1,0:T(8,128)} %fusion, f32[7,1,4,128,128]{4,3,2,1,0:T(8,128)S(1)} %copy-done.3), kind=kOutput, calls=%fused_computation.29 | convolution fusion | flops 1207959552 | bytes 6553600 | tf_op jit(solution)/shard_map/bkj,bjc->bkc/dot_general | solution.py:21
  29.6 0.0 copy-done.2
  29.6 6.0 %convolution_add_fusion.6 = f32[4,1536,128]{2,1,0:T(8,128)S(1)} fusion(f32[4,1536,128]{2,1,0:T(8,128)S(1)} %fusion.22, f32[4,128,1536]{2,1,0:T(8,128)S(1)} %bitcast.87, f32[7,1,4,128,128]{4,3,2,1,0:T(8,128)} %param.8), kind=kOutput, calls=%fused_computation.8 | convolution fusion | flops 1208745984 | bytes 9699328 | tf_op jit(solution)/shard_map/bkj,bjc->bkc/dot_general | solution.py:29
  35.7 0.0 copy-start.1
  35.7 4.6 fusion.19
  40.3 0.0 copy-done.1
  40.3 3.8 rev.7
  44.1 5.0 convolution_add_fusion.5
  49.1 0.0 copy-start.4
  49.1 2.5 collective-permute-start
  51.6 3.0 fusion.16
  54.6 64.8 %collective-permute-done = f32[4,128,1536]{1,2,0:T(8,128)S(1)} collective-permute-done((f32[4,128,1536]{1,2,0:T(8,128)S(1)}, f32[4,128,1536]{1,2,0:T(8,128)S(1)}, u32[]{:S(2)}, u32[]{:S(2)}) %collective-permute-start) | collective-permute-done | bytes 3145760 | tf_op jit(solution)/shard_map/ppermute | solution.py:10
  119.4 0.0 copy-done.4
  119.4 3.1 convolution_add_fusion.4
  122.5 3.4 collective-permute-start.1
  125.9 3.0 fusion.13
  128.9 63.9 %collective-permute-done.1 = f32[4,128,1536]{1,2,0:T(8,128)S(1)} collective-permute-done((f32[4,128,1536]{1,2,0:T(8,128)S(1)}, f32[4,128,1536]{1,2,0:T(8,128)S(1)}, u32[]{:S(2)}, u32[]{:S(2)}) %collective-permute-start.1) | collective-permute-done | bytes 3145760 | tf_op jit(solution)/shard_map/ppermute | solution.py:10
  192.8 3.1 convolution_add_fusion.3
  195.9 2.8 collective-permute-start.2
  198.7 3.0 fusion.10
  201.7 63.2 %collective-permute-done.2 = f32[4,128,1536]{1,2,0:T(8,128)S(1)} collective-permute-done((f32[4,128,1536]{1,2,0:T(8,128)S(1)}, f32[4,128,1536]{1,2,0:T(8,128)S(1)}, u32[]{:S(2)}, u32[]{:S(2)}) %collective-permute-start.2) | collective-permute-done | bytes 3145760 | tf_op jit(solution)/shard_map/ppermute | solution.py:10
  264.9 3.1 convolution_add_fusion.2
  268.0 1.6 collective-permute-start.3
  269.6 3.0 fusion.7
  272.6 62.2 %collective-permute-done.3 = f32[4,128,1536]{1,2,0:T(8,128)S(1)} collective-permute-done((f32[4,128,1536]{1,2,0:T(8,128)S(1)}, f32[4,128,1536]{1,2,0:T(8,128)S(1)}, u32[]{:S(2)}, u32[]{:S(2)}) %collective-permute-start.3) | collective-permute-done | bytes 3145760 | tf_op jit(solution)/shard_map/ppermute | solution.py:10
  334.8 3.1 convolution_add_fusion.1
  337.9 3.0 collective-permute-start.4
  340.9 3.0 fusion.4
  343.9 61.1 %collective-permute-done.4 = f32[4,128,1536]{1,2,0:T(8,128)S(1)} collective-permute-done((f32[4,128,1536]{1,2,0:T(8,128)S(1)}, f32[4,128,1536]{1,2,0:T(8,128)S(1)}, u32[]{:S(2)}, u32[]{:S(2)}) %collective-permute-start.4) | collective-permute-done | bytes 3145760 | tf_op jit(solution)/shard_map/ppermute | solution.py:10
  405.0 3.1 convolution_add_fusion
  408.1 0.0 copy-done
  408.1 12.6 %fusion.38 = f32[4,1536,512]{1,2,0:T(8,128)} fusion(f32[4,1536,128]{2,1,0:T(8,128)S(1)} %convolution_add_fusion, f32[4,512,128]{2,1,0:T(8,128)S(1)} %copy-done), kind=kOutput, calls=%fused_computation.45 | convolution fusion | flops 4831838208 | bytes 16777216 | tf_op jit(solution)/shard_map/bpk,bkc->cbp/dot_general | solution.py:34
  420.7 12.8 %copy.8 = f32[1536,2048]{1,0:T(8,128)} copy(f32[1536,2048]{0,1:T(8,128)} %bitcast.79) | data formatting | bytes 25165824 | tf_op jit(solution)/shard_map/reshape | solution.py:36
  433.5 0.0 reduce-scatter.2.cloned.1.call-update
  433.5 118.6 %reduce-scatter.2.cloned.1.call-done = f32[384,2048]{1,0:T(8,128)} async-done(((f32[1536,2048]{1,0:T(8,128)}), f32[384,2048]{1,0:T(8,128)}) %reduce-scatter.2.cloned.1.call-update) | async-done | bytes 3145744 | tf_op jit(solution)/shard_map/reduce_scatter | solution.py:35
Async XLA Ops:
  6.5 401.6 %copy-start = (f32[4,512,128]{2,1,0:T(8,128)S(1)}, f32[4,512,128]{2,1,0:T(8,128)}, u32[]{:S(2)}) copy-start(f32[4,512,128]{2,1,0:T(8,128)} %param.9) | copy-start | bytes 3145732
  6.5 545.6 %reduce-scatter.2.cloned.1.call-start = ((), (), s32[]{:S(2)}) async-start(), calls=%async_computation.1 | async-start | bytes 15728640 | tf_op jit(solution)/shard_map/reduce_scatter | solution.py:35
  18.6 3.9 copy-start.3
  22.5 7.2 %copy-start.2 = (f32[2,2,1,128,1536]{4,3,1,0,2:T(8,128)S(1)}, f32[2,2,1,128,1536]{4,3,1,0,2:T(8,128)}, u32[]{:S(2)}) copy-start(f32[2,2,1,128,1536]{4,3,1,0,2:T(8,128)} %rev.6) | copy-start | bytes 9437188
  35.7 4.6 copy-start.1
  49.1 70.4 %copy-start.4 = (f32[7,1,4,128,128]{4,3,2,1,0:T(8,128)S(1)}, f32[7,1,4,128,128]{4,3,2,1,0:T(8,128)}, u32[]{:S(2)}) copy-start(f32[7,1,4,128,128]{4,3,2,1,0:T(8,128)} %param.8) | copy-start | bytes 5505028
  49.1 70.4 %collective-permute-start = (f32[4,128,1536]{1,2,0:T(8,128)S(1)}, f32[4,128,1536]{1,2,0:T(8,128)S(1)}, u32[]{:S(2)}, u32[]{:S(2)}) collective-permute-start(f32[4,128,1536]{1,2,0:T(8,128)S(1)} %bitcast.82), channel_id=1, source_target_pairs={{0,1},{1,0},{2,3},{3,2},{4,5},{5,4},{6,7},{7,6},{8,9},{9,8},{10,11... | collective-permute-start | bytes 9437192 | tf_op jit(solution)/shard_map/ppermute | solution.py:10
  122.5 70.3 %collective-permute-start.1 = (f32[4,128,1536]{1,2,0:T(8,128)S(1)}, f32[4,128,1536]{1,2,0:T(8,128)S(1)}, u32[]{:S(2)}, u32[]{:S(2)}) collective-permute-start(f32[4,128,1536]{1,2,0:T(8,128)S(1)} %bitcast.83), channel_id=1, source_target_pairs={{0,2},{1,3},{2,0},{3,1},{4,6},{5,7},{6,4},{7,5},{8,10},{9,11},{10,... | collective-permute-start | bytes 9437192 | tf_op jit(solution)/shard_map/ppermute | solution.py:10
  195.9 69.0 %collective-permute-start.2 = (f32[4,128,1536]{1,2,0:T(8,128)S(1)}, f32[4,128,1536]{1,2,0:T(8,128)S(1)}, u32[]{:S(2)}, u32[]{:S(2)}) collective-permute-start(f32[4,128,1536]{1,2,0:T(8,128)S(1)} %bitcast.84), channel_id=1, source_target_pairs={{0,4},{1,5},{2,6},{3,7},{4,0},{5,1},{6,2},{7,3},{8,12},{9,13},{10,... | collective-permute-start | bytes 9437192 | tf_op jit(solution)/shard_map/ppermute | solution.py:10
  268.0 66.8 %collective-permute-start.3 = (f32[4,128,1536]{1,2,0:T(8,128)S(1)}, f32[4,128,1536]{1,2,0:T(8,128)S(1)}, u32[]{:S(2)}, u32[]{:S(2)}) collective-permute-start(f32[4,128,1536]{1,2,0:T(8,128)S(1)} %bitcast.85), channel_id=1, source_target_pairs={{0,8},{1,9},{2,10},{3,11},{4,12},{5,13},{6,14},{7,15},{8,0},{9,1},... | collective-permute-start | bytes 9437192 | tf_op jit(solution)/shard_map/ppermute | solution.py:10
  337.9 67.1 %collective-permute-start.4 = (f32[4,128,1536]{1,2,0:T(8,128)S(1)}, f32[4,128,1536]{1,2,0:T(8,128)S(1)}, u32[]{:S(2)}, u32[]{:S(2)}) collective-permute-start(f32[4,128,1536]{1,2,0:T(8,128)S(1)} %bitcast.86), channel_id=1, source_target_pairs={{0,16},{1,17},{2,18},{3,19},{4,20},{5,21},{6,22},{7,23},{8,24},{9,... | collective-permute-start | bytes 9437192 | tf_op jit(solution)/shard_map/ppermute | solution.py:10
Sparse Core Ops, SparseCore 0:
  433.6 118.4 reduce-scatter.1
where the time goes:
time: 563 us; the launch traced here: 559 us
  waiting for transfers between devices  434 us (77%)
  matrix products  77.8 us (14%)
  local copies, waits for them, and re-layouts  20.4 us (4%)
  between operations  14 us (2%)
  starting transfers between devices  13.4 us (2%)
    ppermute x5, waiting for transfers between devices, from_partner(): return lax.ppermute(value, axis, pairs)  315 us
    reduce_scatter x1, waiting for transfers between devices, shards(): lax.psum_scatter(terms.reshape(lax.axis_size('shot') * columns_dev, box_d...  119 us
    dot_general x7, matrix products, shards(): jnp.einsum('bkj,bjc->bkc', self_maps[level, 0], coef, precision=highest)  26.7 us
    dot_general x7, matrix products, shards(): jnp.einsum('bkj,bjc->bkc', cross_maps[level, 0], partner, precision=highest)  26.4 us
    ppermute x5, starting transfers between devices, from_partner(): return lax.ppermute(value, axis, pairs)  13.4 us
    reshape x1, local copies, waits for them, and re-layouts, shards(): terms.reshape(lax.axis_size('shot') * columns_dev, box_dev * pixels)  12.8 us
    dot_general x1, matrix products, shards(): terms = jnp.einsum('bpk,bkc->cbp', evaluate, coef, precision=highest)  12.6 us
    dot_general x1, matrix products, shards(): jnp.einsum('bkq,bqc->bkc', first_maps[0], samples[0], precision=highest)  12 us
  transfers between devices with their start and end apart: 6, of which 6 were waited for; matrix products, arithmetic and copies ran while one was open for 3% of the time, Pallas kernels for 0%

commit v1 on v0

v1 whole, which is shorter than its diff:
```python
import functools

import jax
import jax.numpy as jnp
from jax import lax
from jax.experimental import pallas as pl
from jax.experimental.pallas import tpu as pltpu
from jax.sharding import PartitionSpec as P

F32, BF16 = jnp.float32, jnp.bfloat16
MESH = pl.DeviceIdType.MESH

BOX = 4
K = 128
Q = 512
COLS = 1536
SHOTS = 4
CHUNKS = 12
GROUPS = 3
PER_GROUP = CHUNKS // GROUPS
HALF = COLS // CHUNKS // 2
W = HALF // SHOTS
LAG = {"first": 0} | {
    name: PER_GROUP + lag
    for name, lag in dict(local=0, z0=1, z1=2, swap=3, x=4, y1=5, core=6, xlo=7, done=8).items()
}


def split(value):
    high = value.astype(BF16)
    return high, (value - high.astype(F32)).astype(BF16)


def dot(a, b):
    return jnp.dot(a, b, preferred_element_type=F32)


def flip(index, mask):
    return index + mask - 2 * mask * ((index // mask) % 2)


def kernel(
    samples, first, selfs, crosses, out,
    smp, fst, fst2, own, got, wt, c0, r1, d2, r2, d3, r3, r4, r6, rc, gx, rx, fin,
    sem_in, sem_map, map_send, map_recv, send, recv,
):
    shot, b = lax.axis_index("shot"), lax.axis_index("bfly")
    core, xlo = shot % 2, shot // 2
    half = (b % 2 + (b // 2) % 2 + (b // 8) % 2 + (b // 16) % 2) % 2

    def peer(mask):
        at = b
        for bit in (1, 2, 4, 8, 16):
            if mask & bit:
                at = flip(at, bit)
        return (shot, at)

    to_z0, to_z1, to_swap, to_x, to_y0, to_y1 = (peer(m) for m in (1, 3, 9, 4, 8, 24))
    to_core, to_xlo = (flip(shot, 1), b), (flip(shot, 2), b)
    peers = (to_z0, to_z1, to_swap, to_x, to_y0, to_y1, to_core, to_xlo)

    def load(i):
        g, s = i // SHOTS, i % SHOTS
        at = pl.multiple_of(s * (COLS // SHOTS) + g * 128, 128)
        return pltpu.make_async_copy(samples.at[0, :, :, pl.ds(at, 128)], smp.at[i], sem_in.at[i])

    first_load = pltpu.make_async_copy(first.at[0], fst, sem_map.at[0])
    self_load = pltpu.make_async_copy(selfs.at[:, 0], own.at[0], sem_map.at[1])
    cross_load = pltpu.make_async_copy(crosses.at[:, 0], own.at[1], sem_map.at[2])
    first_load.start()

    def start_load(i, carry):
        load(i).start()
        return carry

    lax.fori_loop(0, SHOTS, start_load, 0)
    self_load.start()
    cross_load.start()
    lax.fori_loop(SHOTS, GROUPS * SHOTS, start_load, 0)

    barrier = pltpu.get_barrier_semaphore()
    for device in peers:
        pl.semaphore_signal(barrier, inc=1, device_id=device, device_id_type=MESH)
    pl.semaphore_wait(barrier, len(peers))

    def remote(src, dst, phase, i, device):
        return pltpu.make_async_remote_copy(
            src_ref=src, dst_ref=dst, send_sem=send.at[phase, i], recv_sem=recv.at[phase, i],
            device_id=device, device_id_type=MESH,
        )

    def map_copies(level):
        device = to_z0 if level < 4 else to_y0
        return [
            pltpu.make_async_remote_copy(
                src_ref=ref.at[level, 0], dst_ref=got.at[n, level - 2],
                send_sem=map_send.at[n, level - 2], recv_sem=map_recv.at[n, level - 2],
                device_id=device, device_id_type=MESH,
            )
            for n, ref in enumerate((selfs, crosses))
        ]

    def start_maps(level):
        for copy in map_copies(level):
            copy.start()

    def wait_maps(level):
        for copy in map_copies(level):
            copy.wait()

    def p_z0(i):
        return remote(c0.at[i, 1 - half], r1.at[i], 0, i, to_z0)

    def p_z1(i):
        return remote(d2.at[i], r2.at[i], 1, i, to_z1)

    def p_swap(i):
        return remote(d3.at[i, 1], r3.at[i], 2, i, to_swap)

    def p_x(i, slot):
        return remote(d3.at[i, 0] if slot == 0 else r3.at[i], r4.at[i, slot], 3 + slot, i, to_x)

    def p_y1(i):
        return remote(d2.at[i], r6.at[i], 5, i, to_y1)

    def p_core(i):
        return remote(d3.at[i, :, :, pl.ds(pl.multiple_of((1 - core) * 2 * W, 2 * W), 2 * W)], rc.at[i], 6, i, to_core)

    def p_xlo(i):
        return remote(gx.at[i], rx.at[i], 7, i, to_xlo)

    def rows_of(i, h):
        return pl.ds(pl.multiple_of((2 * i + h) * W, W), W)

    def p_join(i):
        return remote(d3.at[i, 1, :, pl.ds(0, W)], fin.at[:, rows_of(i, half)], 8, i, to_y0)

    def pair_weights(tile, si, ci, sj, cj):
        for (row, col), m in {(0, 0): si, (1, 0): ci, (0, 1): cj, (1, 1): sj}.items():
            high, low = split(m.T)
            wt[tile, pl.ds(row * K, K), pl.ds(col * K, K)] = high
            wt[tile + 1, pl.ds(row * K, K), pl.ds(col * K, K)] = low

    def direct_weights(tile, s, c):
        for row, m in enumerate((s, c)):
            high, low = split(m.T)
            wt[tile, pl.ds(row * K, K), pl.ds(0, K)] = high
            wt[tile, pl.ds(row * K, K), pl.ds(K, K)] = low

    def prepare_local():
        for level in (0, 1):
            for p in range(2):
                i, j = ((2 * p, 2 * p + 1), (p, p + 2))[level]
                pair_weights(4 * level + 2 * p, own[0, level, i], own[1, level, i], own[0, level, j], own[1, level, j])

    def prepare(level):
        wait_maps(level)
        base = 8 * (level - 1)

        def one(box, carry):
            mine = own[0, level, box], own[1, level, box]
            other = got[0, level - 2, box], got[1, level - 2, box]
            if level in (2, 5):
                pair_weights(base + 2 * box, *mine, *other)
            else:
                direct_weights(base + box, *mine)
                direct_weights(base + BOX + box, *other)
            return carry

        lax.fori_loop(0, BOX, one, 0)

    def pair(tile, xi, xj):
        high, low = split(jnp.concatenate([xi, xj], axis=1))
        y = dot(high, wt[tile]) + dot(low, wt[tile]) + dot(high, wt[tile + 1])
        return y[:, :K], y[:, K:]

    def direct(tile, x, partner):
        high, low = split(jnp.concatenate([x, partner], axis=1))
        y = dot(high, wt[tile])
        return y[:, :K] + y[:, K:] + dot(low, wt[tile, :, pl.ds(0, K)])

    def stage_first(i):
        load(i).wait()
        g, s = i // SHOTS, i % SHOTS
        row = pl.multiple_of(((s % 2) * 2 + s // 2) * W, W)

        def one(box, carry):
            high, low = split(smp[i, box])
            y = dot(fst2[box], high)
            y = y[:K] + y[K:] + dot(fst2[box, pl.ds(0, K)], low)
            y = y.T
            for part in range(PER_GROUP):
                for h in range(2):
                    c0[g * PER_GROUP + part, h, box, pl.ds(row, W)] = y[(2 * part + h) * W : (2 * part + h + 1) * W]
            return carry

        lax.fori_loop(0, BOX, one, 0)

    def stage_local(i):
        x = [c0[i, :, box].reshape(2 * HALF, K) for box in range(BOX)]
        x[0], x[1] = pair(0, x[0], x[1])
        x[2], x[3] = pair(2, x[2], x[3])
        x[0], x[2] = pair(4, x[0], x[2])
        x[1], x[3] = pair(6, x[1], x[3])
        for box in range(BOX):
            c0[i, :, box] = x[box].reshape(2, HALF, K)
        p_z0(i).start()

    def stage_z0(i):
        p_z0(i).wait()
        for box in range(BOX):
            d2[i, 0, box], d2[i, 1, box] = pair(8 + 2 * box, c0[i, half, box], r1[i, box])
        p_z1(i).start()

    def stage_z1(i):
        p_z1(i).wait()
        for box in range(BOX):
            d3[i, 1, box] = direct(16 + BOX + box, d2[i, 1, box], r2[i, 0, box])
        p_swap(i).start()
        for box in range(BOX):
            d3[i, 0, box] = direct(16 + box, d2[i, 0, box], r2[i, 1, box])
        p_x(i, 0).start()

    def stage_swap(i):
        p_swap(i).wait()
        p_x(i, 1).start()

    def stage_x(i):
        p_x(i, 0).wait()
        p_x(i, 1).wait()
        for box in range(BOX):
            x0 = direct(24 + box, d3[i, 0, box], r4[i, 0, box])
            x1 = direct(24 + BOX + box, r3[i, box], r4[i, 1, box])
            d2[i, 0, box], d2[i, 1, box] = pair(32 + 2 * box, x0, x1)
        p_y1(i).start()

    def stage_y1(i):
        p_y1(i).wait()
        for slot in range(2):
            for box in range(BOX):
                d3[i, slot, box] = direct(40 + slot * BOX + box, d2[i, slot, box], r6[i, 1 - slot, box])
        p_core(i).start()

    def stage_core(i):
        p_core(i).wait()
        away = pl.multiple_of(core * 2 * W + (1 - xlo) * W, W)
        gx[i] = d3[i, :, :, pl.ds(away, W)] + rc[i, :, :, pl.ds(pl.multiple_of((1 - xlo) * W, W), W)]
        p_xlo(i).start()

    def stage_xlo(i):
        p_xlo(i).wait()
        stay = pl.multiple_of(core * 2 * W + xlo * W, W)
        total = d3[i, :, :, pl.ds(stay, W)] + rc[i, :, :, pl.ds(pl.multiple_of(xlo * W, W), W)] + rx[i]
        fin[:, rows_of(i, half)] = total[0]
        d3[i, 1, :, pl.ds(0, W)] = total[1]
        p_join(i).start()

    def stage_done(i):
        p_join(i).wait()

    start_maps(2)
    start_maps(4)
    first_load.wait()
    for box in range(BOX):
        high, low = split(fst[box])
        fst2[box, pl.ds(0, K)] = high
        fst2[box, pl.ds(K, K)] = low

    prepares = {"local": (), "z0": (2,), "z1": (3,), "x": (4, 5), "y1": (6,)}
    stages = dict(
        first=stage_first, local=stage_local, z0=stage_z0, z1=stage_z1, swap=stage_swap, x=stage_x,
        y1=stage_y1, core=stage_core, xlo=stage_xlo, done=stage_done,
    )

    def tick(t, carry):
        for name, stage in stages.items():
            i = t - LAG[name]

            if name in prepares:

                @pl.when(i == 0)
                def _(name=name):
                    if name == "local":
                        self_load.wait()
                        cross_load.wait()
                        prepare_local()
                    for level in prepares[name]:
                        prepare(level)

            @pl.when(jnp.logical_and(i >= 0, i < CHUNKS))
            def _(stage=stage, i=i):
                stage(i)

            if name == "local":

                @pl.when(i == 0)
                def _():
                    for level in (3, 5, 6):
                        start_maps(level)

        return carry

    lax.fori_loop(0, CHUNKS + LAG["done"], tick, 0)
    out[...] = fin[...]


def evaluate_kernel(coef, evaluate, image):
    xh, xl = split(coef[0])
    eh, el = split(evaluate[0])
    nt = (((1,), (1,)), ((), ()))
    y = lax.dot_general(xh, eh, nt, preferred_element_type=F32)
    y += lax.dot_general(xl, eh, nt, preferred_element_type=F32)
    y += lax.dot_general(xh, el, nt, preferred_element_type=F32)
    image[...] = y


def shards(samples, first_maps, self_maps, cross_maps, evaluate):
    n = CHUNKS
    vmem = pltpu.VMEM
    any_space = pl.BlockSpec(memory_space=pl.ANY)
    rows = COLS // SHOTS
    coef = pl.pallas_call(
        kernel,
        out_shape=jax.ShapeDtypeStruct((BOX, rows, K), F32),
        in_specs=[any_space] * 4,
        out_specs=pl.BlockSpec(memory_space=pltpu.VMEM),
        scratch_shapes=[
            vmem((GROUPS * SHOTS, BOX, Q, 128), F32),
            vmem((BOX, K, Q), F32),
            vmem((BOX, 2 * K, Q), BF16),
            vmem((2, 7, BOX, K, K), F32),
            vmem((2, 5, BOX, K, K), F32),
            vmem((48, 2 * K, 2 * K), BF16),
            vmem((n, 2, BOX, HALF, K), F32),
            vmem((n, BOX, HALF, K), F32),
            vmem((n, 2, BOX, HALF, K), F32),
            vmem((n, 2, BOX, HALF, K), F32),
            vmem((n, 2, BOX, HALF, K), F32),
            vmem((n, BOX, HALF, K), F32),
            vmem((n, 2, BOX, HALF, K), F32),
            vmem((n, 2, BOX, HALF, K), F32),
            vmem((n, 2, BOX, 2 * W, K), F32),
            vmem((n, 2, BOX, W, K), F32),
            vmem((n, 2, BOX, W, K), F32),
            vmem((BOX, rows, K), F32),
            pltpu.SemaphoreType.DMA((GROUPS * SHOTS,)),
            pltpu.SemaphoreType.DMA((3,)),
            pltpu.SemaphoreType.DMA((2, 5)),
            pltpu.SemaphoreType.DMA((2, 5)),
            pltpu.SemaphoreType.DMA((9, n)),
            pltpu.SemaphoreType.DMA((9, n)),
        ],
        compiler_params=pltpu.CompilerParams(
            collective_id=0, has_side_effects=True, vmem_limit_bytes=60 * 2**20
        ),
    )(samples, first_maps, self_maps, cross_maps)
    pixels = evaluate.shape[1]
    return pl.pallas_call(
        evaluate_kernel,
        grid=(BOX,),
        out_shape=jax.ShapeDtypeStruct((rows, BOX * pixels), F32),
        in_specs=[
            pl.BlockSpec((1, rows, K), lambda i: (i, 0, 0)),
            pl.BlockSpec((1, pixels, K), lambda i: (i, 0, 0)),
        ],
        out_specs=pl.BlockSpec((rows, pixels), lambda i: (0, i)),
    )(coef, evaluate)


def solution(mesh):
    in_specs = (
        P("shot", "bfly", None, None),
        P("shot", "bfly", None, None),
        P(None, "shot", "bfly", None, None),
        P(None, "shot", "bfly", None, None),
        P("bfly", None, None),
    )
    out_specs = P("shot", "bfly")
    return jax.shard_map(shards, mesh=mesh, in_specs=in_specs, out_specs=out_specs, check_vma=False)
```

time: 563 us -> 152 us (0.27)
  waiting for transfers between devices: 434 us -> 0 us
  Pallas kernels: 0 us -> 151 us
  matrix products: 77.8 us -> 0 us
  local copies, waits for them, and re-layouts: 20.4 us -> 0 us
  between operations: 14 us -> 0.01 us
  starting transfers between devices: 13.4 us -> 0 us
    ppermute x5 -> x0, waiting for transfers between devices: 315 us -> none  [from_partner(): return lax.ppermute(value, axis, pairs)]
    pallas_call x0 -> x2, Pallas kernels: none -> 151 us  [the longest x1 146 us: shards(): pl.pallas_call(kernel, out_shape=jax.ShapeDtypeStruct((BOX, rows, K), F32...]
    reduce_scatter x1 -> x0, waiting for transfers between devices: 119 us -> none  [shards(): lax.psum_scatter(terms.reshape(lax.axis_size('shot') * columns_dev, box_d...]
    dot_general x16 -> x0, matrix products: 77.8 us -> none  [the longest x7 26.7 us: shards(): jnp.einsum('bkj,bjc->bkc', self_maps[level, 0], coef, precision=highest)]
    ppermute x5 -> x0, starting transfers between devices: 13.4 us -> none  [from_partner(): return lax.ppermute(value, axis, pairs)]
    reshape x1 -> x0, local copies, waits for them, and re-layouts: 12.8 us -> none  [shards(): terms.reshape(lax.axis_size('shot') * columns_dev, box_dev * pixels)]
    rev x2 -> x0, local copies, waits for them, and re-layouts: 7.63 us -> none  [shards(): partner = paired[:, ::-1].reshape(shape)]
  transfers between devices with their start and end apart: 6 -> 0, of which waited for: 6 -> 0; matrix products, arithmetic and copies ran while one was open for 3% -> 0% of each run, Pallas kernels for 0% -> 0%
where the time goes in v1:
time: 152 us; the launch traced here: 151 us
  Pallas kernels  151 us (99%)
    pallas_call x1, Pallas kernels, shards(): pl.pallas_call(kernel, out_shape=jax.ShapeDtypeStruct((BOX, rows, K), F32...  146 us
    pallas_call x1, Pallas kernels, shards(): pl.pallas_call(evaluate_kernel, grid=(BOX,), out_shape=jax.ShapeDtypeStru...  4.85 us

profile of v1, /device:TPU:1, one launch (start us, length us, event | category | flops | bytes accessed | tf_op | source)
XLA Modules:
  0.0 151.1 jit_solution(13254212147594254422)
XLA Ops:
  0.0 146.3 %shard_map.55.coef = f32[4,384,128]{2,1,0:T(8,128)} custom-call(f32[1,4,512,1536]{3,2,1,0:T(8,128)} %samples.1, f32[1,4,128,512]{3,2,1,0:T(8,128)} %first.1, f32[7,1,4,128,128]{4,3,2,1,0:T(8,128)} %selfs.1, f32[7,1,4,128,128]{4,3,2,1,0:T(8,128)} %crosses.1), custom_call_target="tpu_custom_call" | custom-call | tf_op jit(solution)/shard_map/pallas_call | solution.py:322
  146.3 4.9 %shard_map.56 = f32[384,2048]{1,0:T(8,128)} custom-call(f32[4,384,128]{2,1,0:T(8,128)} %shard_map.55.coef, f32[4,512,128]{2,1,0:T(8,128)} %evaluate.1), custom_call_target="tpu_custom_call" | custom-call | tf_op jit(solution)/shard_map/pallas_call | solution.py:358

commit v2 on v1

v2 whole, which is shorter than its diff:
```python
import functools

import jax
import jax.numpy as jnp
from jax import lax
from jax.experimental import pallas as pl
from jax.experimental.pallas import tpu as pltpu
from jax.sharding import PartitionSpec as P

F32, BF16 = jnp.float32, jnp.bfloat16
MESH = pl.DeviceIdType.MESH

BOX = 4
K = 128
Q = 512
COLS = 1536
SHOTS = 4
CHUNKS = 24
GROUPS = 3
PER_GROUP = CHUNKS // GROUPS
WIDTH = COLS // CHUNKS
W = WIDTH // SHOTS
LAG = {"first": 0} | {
    name: PER_GROUP + lag for name, lag in dict(local=0, z=5, swap=8, y1=12, core=13, xlo=15, done=18).items()
}
ORDER = ("local", "xlo", "core", "swap", "z", "done", "y1", "first")
IN_Z = {1: 1, 2: 2, 3: 3}
SWAP = {1: 9, 2: 6, 3: 15}
HOME = {1: 8, 2: 4, 3: 12}
Y1 = 24
A2A, SWAPPED, DIRECT, CORE, XLO, JOIN, PHASES = 0, 3, 6, 7, 8, 9, 12


def split(value):
    high = value.astype(BF16)
    return high, (value - high.astype(F32)).astype(BF16)


def dot(a, b):
    return jnp.dot(a, b, preferred_element_type=F32)


def x_rows(x):
    return x.shape[0]


def flip(index, mask):
    for bit in (1, 2, 4, 8, 16):
        if mask & bit:
            index = index + bit - 2 * bit * ((index // bit) % 2)
    return index


def kernel(
    samples, first, selfs, crosses, out,
    smp, fst, fst2, own, got, wt, c0, r1, d2, r3, d5, r6, d6, rc, gx, rx, fin,
    sem_in, sem_map, map_send, map_recv, send, recv,
):
    shot, b = lax.axis_index("shot"), lax.axis_index("bfly")
    core, xlo = shot % 2, shot // 2
    bit = [(b // 2**n) % 2 for n in range(5)]
    mine = 2 * ((bit[1] + bit[2]) % 2) + (bit[0] + bit[3] + bit[4]) % 2

    def peer(mask):
        return (shot, flip(b, mask))

    to_core, to_xlo = (flip(shot, 1), b), (flip(shot, 2), b)
    masks = sorted({*IN_Z.values(), *SWAP.values(), *HOME.values(), Y1})
    peers = [peer(mask) for mask in masks] + [to_core, to_xlo]

    def load(i):
        g, s = i // SHOTS, i % SHOTS
        at = pl.multiple_of(s * (COLS // SHOTS) + g * 128, 128)
        return pltpu.make_async_copy(samples.at[0, :, :, pl.ds(at, 128)], smp.at[i], sem_in.at[i])

    first_load = pltpu.make_async_copy(first.at[0], fst, sem_map.at[0])
    self_load = pltpu.make_async_copy(selfs.at[:, 0], own.at[0], sem_map.at[1])
    cross_load = pltpu.make_async_copy(crosses.at[:, 0], own.at[1], sem_map.at[2])
    first_load.start()

    def start_load(i, carry):
        load(i).start()
        return carry

    lax.fori_loop(0, SHOTS, start_load, 0)
    self_load.start()
    cross_load.start()
    lax.fori_loop(SHOTS, GROUPS * SHOTS, start_load, 0)

    barrier = pltpu.get_barrier_semaphore()
    for device in peers:
        pl.semaphore_signal(barrier, inc=1, device_id=device, device_id_type=MESH)
    pl.semaphore_wait(barrier, len(peers))

    def remote(src, dst, phase, i, device):
        return pltpu.make_async_remote_copy(
            src_ref=src, dst_ref=dst, send_sem=send.at[phase, i], recv_sem=recv.at[phase, i],
            device_id=device, device_id_type=MESH,
        )

    def map_copies(level):
        return [
            pltpu.make_async_remote_copy(
                src_ref=ref.at[level, 0, flip(mine, k)], dst_ref=got.at[n, level - 2, k - 1],
                send_sem=map_send.at[n, level - 2, k - 1], recv_sem=map_recv.at[n, level - 2, k - 1],
                device_id=peer((IN_Z if level < 4 else HOME)[k]), device_id_type=MESH,
            )
            for n, ref in enumerate((selfs, crosses))
            for k in (1, 2, 3)
        ]

    def start_maps(level):
        for copy in map_copies(level):
            copy.start()

    def wait_maps(level):
        for copy in map_copies(level):
            copy.wait()

    def p_z(i, k):
        return remote(c0.at[i, flip(mine, k)], r1.at[i, k - 1], A2A + k - 1, i, peer(IN_Z[k]))

    def p_swap(i, k):
        return remote(d2.at[i, k], r3.at[i, k - 1], SWAPPED + k - 1, i, peer(SWAP[k]))

    def p_y1(i):
        return remote(d5.at[i], r6.at[i], DIRECT, i, peer(Y1))

    def p_core(i):
        rows = pl.ds(pl.multiple_of((1 - core) * 2 * W, 2 * W), 2 * W)
        return remote(d6.at[i, :, rows], rc.at[i], CORE, i, to_core)

    def p_xlo(i):
        return remote(gx.at[i], rx.at[i], XLO, i, to_xlo)

    def rows_of(i):
        return pl.ds(pl.multiple_of(i * W, W), W)

    def p_join(i, k):
        return remote(gx.at[i, k], fin.at[mine, rows_of(i)], JOIN + k - 1, i, peer(HOME[k]))

    def pair_weights(tile, si, ci, sj, cj):
        for (row, col), m in {(0, 0): si, (1, 0): ci, (0, 1): cj, (1, 1): sj}.items():
            high, low = split(m.T)
            wt[tile, pl.ds(row * K, K), pl.ds(col * K, K)] = high
            wt[tile + 1, pl.ds(row * K, K), pl.ds(col * K, K)] = low

    def direct_weights(tile, s, c):
        for row, m in enumerate((s, c)):
            high, low = split(m.T)
            wt[tile, pl.ds(row * K, K), pl.ds(0, K)] = high
            wt[tile, pl.ds(row * K, K), pl.ds(K, K)] = low

    near, far = ((0, 1), (2, 3)), ((0, 2), (1, 3))
    pairs = {0: near, 1: far, 2: near, 3: far, 4: far, 5: near}

    def maps_of(level, slot):
        if level < 2:
            return own[0, level, slot], own[1, level, slot]
        if slot == 0:
            return own[0, level, mine], own[1, level, mine]
        return got[0, level - 2, slot - 1], got[1, level - 2, slot - 1]

    def prepare(level):
        if level >= 2:
            wait_maps(level)
        if level in pairs:
            for p, (i, j) in enumerate(pairs[level]):
                pair_weights(4 * level + 2 * p, *maps_of(level, i), *maps_of(level, j))
        else:
            for slot in range(4):
                direct_weights(4 * level + slot, *maps_of(level, slot))

    def pair(tile, xi, xj):
        high, low = split(jnp.concatenate([xi, xj], axis=1))
        y = dot(jnp.concatenate([high, low], axis=0), wt[tile])
        y = y[: x_rows(xi)] + y[x_rows(xi) :] + dot(high, wt[tile + 1])
        return y[:, :K], y[:, K:]

    def apply(level, x):
        x = list(x)
        for p, (i, j) in enumerate(pairs[level]):
            x[i], x[j] = pair(4 * level + 2 * p, x[i], x[j])
        return x

    def direct(tile, x, partner):
        high, low = split(jnp.concatenate([x, partner], axis=1))
        y = dot(jnp.concatenate([high, low], axis=0), wt[tile])
        return y[: x_rows(x), :K] + y[: x_rows(x), K:] + y[x_rows(x) :, :K]

    def stage_first(t):
        if CHUNKS > GROUPS * SHOTS:
            every = CHUNKS // (GROUPS * SHOTS)

            @pl.when(t % every == 0)
            def _():
                first_block(t // every)
        else:
            several = GROUPS * SHOTS // CHUNKS
            for n in range(several):
                first_block(t * several + n)

    def first_block(i):
        load(i).wait()
        g, s = i // SHOTS, i % SHOTS
        row = pl.multiple_of(((s % 2) * 2 + s // 2) * W, W)

        def one(box, carry):
            high, low = split(smp[i, box])
            y = dot(fst2[box], jnp.concatenate([high, low], axis=1))
            y = (y[:K, :K] + y[K:, :K] + y[:K, K:]).T
            for part in range(PER_GROUP):
                c0[g * PER_GROUP + part, box, pl.ds(row, W)] = y[part * W : (part + 1) * W]
            return carry

        lax.fori_loop(0, BOX, one, 0)

    def stage_local(i):
        x = apply(1, apply(0, [c0[i, box] for box in range(BOX)]))
        for box in range(BOX):
            c0[i, box] = x[box]
        for k in (1, 2, 3):
            p_z(i, k).start()

    def stage_z(i):
        for k in (1, 2, 3):
            p_z(i, k).wait()
        x = apply(3, apply(2, [c0[i, mine]] + [r1[i, k - 1] for k in (1, 2, 3)]))
        for k in range(4):
            d2[i, k] = x[k]
        for k in (1, 2, 3):
            p_swap(i, k).start()

    def stage_swap(i):
        for k in (1, 2, 3):
            p_swap(i, k).wait()
        x = apply(5, apply(4, [d2[i, 0]] + [r3[i, k - 1] for k in (1, 2, 3)]))
        for k in range(4):
            d5[i, k] = x[k]
        p_y1(i).start()

    def stage_y1(i):
        p_y1(i).wait()
        for k in range(4):
            d6[i, k] = direct(24 + k, d5[i, k], r6[i, k ^ 1])
        p_core(i).start()

    def stage_core(i):
        p_core(i).wait()
        away = pl.multiple_of(core * 2 * W + (1 - xlo) * W, W)
        gx[i] = d6[i, :, pl.ds(away, W)] + rc[i, :, pl.ds(pl.multiple_of((1 - xlo) * W, W), W)]
        p_xlo(i).start()

    def stage_xlo(i):
        p_xlo(i).wait()
        stay = pl.multiple_of(core * 2 * W + xlo * W, W)
        total = d6[i, :, pl.ds(stay, W)] + rc[i, :, pl.ds(pl.multiple_of(xlo * W, W), W)] + rx[i]
        fin[mine, rows_of(i)] = total[0]
        gx[i] = total
        for k in (1, 2, 3):
            p_join(i, k).start()

    def stage_done(i):
        for k in (1, 2, 3):
            p_join(i, k).wait()

    start_maps(2)
    start_maps(4)
    start_maps(3)
    first_load.wait()
    for box in range(BOX):
        high, low = split(fst[box])
        fst2[box, pl.ds(0, K)] = high
        fst2[box, pl.ds(K, K)] = low

    prepares = {"local": (0, 1), "z": (2, 3), "swap": (4, 5), "y1": (6,)}
    stages = dict(
        first=stage_first, local=stage_local, z=stage_z, swap=stage_swap,
        y1=stage_y1, core=stage_core, xlo=stage_xlo, done=stage_done,
    )

    def tick(t, carry):
        for name in ORDER:
            stage = stages[name]
            i = t - LAG[name]

            if name in prepares:

                @pl.when(i == 0)
                def _(name=name):
                    if name == "local":
                        self_load.wait()
                        cross_load.wait()
                    for level in prepares[name]:
                        prepare(level)

            @pl.when(jnp.logical_and(i >= 0, i < CHUNKS))
            def _(stage=stage, i=i):
                stage(i)

            if name == "local":

                @pl.when(i == 0)
                def _():
                    for level in (5, 6):
                        start_maps(level)

        return carry

    lax.fori_loop(0, CHUNKS + LAG["done"], tick, 0)
    out[...] = fin[...]


def evaluate_kernel(coef_in, evaluate_in, image, coef, evaluate, part, sem_coef, sem_evaluate, sem_image):
    pixels = evaluate.shape[1]
    loads = [
        (
            pltpu.make_async_copy(coef_in.at[box], coef.at[box], sem_coef.at[box]),
            pltpu.make_async_copy(evaluate_in.at[box], evaluate.at[box], sem_evaluate.at[box]),
        )
        for box in range(BOX)
    ]
    stores = [
        pltpu.make_async_copy(part.at[box], image.at[:, pl.ds(box * pixels, pixels)], sem_image.at[box])
        for box in range(BOX)
    ]
    for pair in loads:
        for load in pair:
            load.start()
    for box in range(BOX):
        for load in loads[box]:
            load.wait()
        xh, xl = split(coef[box])
        eh, el = split(evaluate[box])
        nt = (((1,), (1,)), ((), ()))
        y = lax.dot_general(
            jnp.concatenate([xh, xl], axis=1), jnp.concatenate([eh, eh], axis=1), nt, preferred_element_type=F32
        )
        part[box] = y + lax.dot_general(xh, el, nt, preferred_element_type=F32)
        stores[box].start()
    for store in stores:
        store.wait()


def shards(samples, first_maps, self_maps, cross_maps, evaluate):
    n = CHUNKS
    vmem = pltpu.VMEM
    any_space = pl.BlockSpec(memory_space=pl.ANY)
    rows = COLS // SHOTS
    coef = pl.pallas_call(
        kernel,
        out_shape=jax.ShapeDtypeStruct((BOX, rows, K), F32),
        in_specs=[any_space] * 4,
        out_specs=pl.BlockSpec(memory_space=pltpu.VMEM),
        scratch_shapes=[
            vmem((GROUPS * SHOTS, BOX, Q, 128), F32),
            vmem((BOX, K, Q), F32),
            vmem((BOX, 2 * K, Q), BF16),
            vmem((2, 7, BOX, K, K), F32),
            vmem((2, 5, 3, K, K), F32),
            vmem((28, 2 * K, 2 * K), BF16),
            vmem((n, 4, WIDTH, K), F32),
            vmem((n, 3, WIDTH, K), F32),
            vmem((n, 4, WIDTH, K), F32),
            vmem((n, 3, WIDTH, K), F32),
            vmem((n, 4, WIDTH, K), F32),
            vmem((n, 4, WIDTH, K), F32),
            vmem((n, 4, WIDTH, K), F32),
            vmem((n, 4, 2 * W, K), F32),
            vmem((n, 4, W, K), F32),
            vmem((n, 4, W, K), F32),
            vmem((BOX, rows, K), F32),
            pltpu.SemaphoreType.DMA((GROUPS * SHOTS,)),
            pltpu.SemaphoreType.DMA((3,)),
            pltpu.SemaphoreType.DMA((2, 5, 3)),
            pltpu.SemaphoreType.DMA((2, 5, 3)),
            pltpu.SemaphoreType.DMA((PHASES, n)),
            pltpu.SemaphoreType.DMA((PHASES, n)),
        ],
        compiler_params=pltpu.CompilerParams(
            collective_id=0, has_side_effects=True, vmem_limit_bytes=60 * 2**20
        ),
    )(samples, first_maps, self_maps, cross_maps)
    pixels = evaluate.shape[1]
    return pl.pallas_call(
        evaluate_kernel,
        out_shape=jax.ShapeDtypeStruct((rows, BOX * pixels), F32),
        in_specs=[any_space] * 2,
        out_specs=any_space,
        scratch_shapes=[
            vmem((BOX, rows, K), F32),
            vmem((BOX, pixels, K), F32),
            vmem((BOX, rows, pixels), F32),
            pltpu.SemaphoreType.DMA((BOX,)),
            pltpu.SemaphoreType.DMA((BOX,)),
            pltpu.SemaphoreType.DMA((BOX,)),
        ],
        compiler_params=pltpu.CompilerParams(vmem_limit_bytes=32 * 2**20),
    )(coef, evaluate)


def solution(mesh):
    in_specs = (
        P("shot", "bfly", None, None),
        P("shot", "bfly", None, None),
        P(None, "shot", "bfly", None, None),
        P(None, "shot", "bfly", None, None),
        P("bfly", None, None),
    )
    out_specs = P("shot", "bfly")
    return jax.shard_map(shards, mesh=mesh, in_specs=in_specs, out_specs=out_specs, check_vma=False)
```

time: 152 us -> 120 us (0.79)
  Pallas kernels: 151 us -> 119 us
    pallas_call x1, Pallas kernels: 146 us -> 115 us  [shards(): pl.pallas_call(kernel, out_shape=jax.ShapeDtypeStruct((BOX, rows, K), F32...]
where the time goes in v2:
time: 120 us
  Pallas kernels  119 us (99%)
    pallas_call x1, Pallas kernels, shards(): pl.pallas_call(kernel, out_shape=jax.ShapeDtypeStruct((BOX, rows, K), F32...  115 us
    pallas_call x1, Pallas kernels, shards(): pl.pallas_call(evaluate_kernel, out_shape=jax.ShapeDtypeStruct((rows, BOX...  3.54 us

profile of v2, /device:TPU:1, one launch (start us, length us, event | category | flops | bytes accessed | tf_op | source)
XLA Modules:
  0.0 119.9 jit_solution(9092910634725991771)
XLA Ops:
  0.0 0.0 copy-start.1
  0.0 115.2 %shard_map.55.coef_in = f32[4,384,128]{2,1,0:T(8,128)} custom-call(f32[1,4,512,1536]{3,2,1,0:T(8,128)} %samples.1, f32[1,4,128,512]{3,2,1,0:T(8,128)} %first.1, f32[7,1,4,128,128]{4,3,2,1,0:T(8,128)} %selfs.1, f32[7,1,4,128,128]{4,3,2,1,0:T(8,128)} %crosses.1), custom_call_target="tpu_custom_call" | custom-call | tf_op jit(solution)/shard_map/pallas_call | solution.py:350
  115.2 0.0 copy-done.1
  115.3 0.0 copy-start
  115.3 1.1 copy-done
  116.4 3.5 %shard_map.56 = f32[384,2048]{1,0:T(8,128)} custom-call(f32[4,384,128]{2,1,0:T(8,128)S(1)} %copy-done, f32[4,512,128]{2,1,0:T(8,128)S(1)} %copy-done.1), custom_call_target="tpu_custom_call" | custom-call | tf_op jit(solution)/shard_map/pallas_call | solution.py:385
Async XLA Ops:
  0.0 115.2 %copy-start.1 = (f32[4,512,128]{2,1,0:T(8,128)S(1)}, f32[4,512,128]{2,1,0:T(8,128)}, u32[]{:S(2)}) copy-start(f32[4,512,128]{2,1,0:T(8,128)} %evaluate_in.1) | copy-start | bytes 3145732
  115.3 1.1 copy-start

commit v3 on v2

--- a/solution.py
+++ b/solution.py
@@ -20,6 +20,7 @@
 PER_GROUP = CHUNKS // GROUPS
 WIDTH = COLS // CHUNKS
 W = WIDTH // SHOTS
+LAST = 2
 LAG = {"first": 0} | {
     name: PER_GROUP + lag for name, lag in dict(local=0, z=5, swap=8, y1=12, core=13, xlo=15, done=18).items()
 }
@@ -53,8 +54,8 @@
 
 def kernel(
     samples, first, selfs, crosses, out,
-    smp, fst, fst2, own, got, wt, c0, r1, d2, r3, d5, r6, d6, rc, gx, rx, fin,
-    sem_in, sem_map, map_send, map_recv, send, recv,
+    smp, fst, fst2, own, got, wt, c0, r1, d2, r3, d5, r6, d6, rc, gx, rx, part, home, fin,
+    sem_in, sem_out, sem_map, map_send, map_recv, send, recv, part_send, part_recv,
 ):
     shot, b = lax.axis_index("shot"), lax.axis_index("bfly")
     core, xlo = shot % 2, shot // 2
@@ -66,7 +67,8 @@
 
     to_core, to_xlo = (flip(shot, 1), b), (flip(shot, 2), b)
     masks = sorted({*IN_Z.values(), *SWAP.values(), *HOME.values(), Y1})
-    peers = [peer(mask) for mask in masks] + [to_core, to_xlo]
+    across = [(flip(shot, 2), b)] + [(flip(shot, 2), flip(b, HOME[k])) for k in (1, 2, 3)]
+    peers = [peer(mask) for mask in masks] + [to_core] + across
 
     def load(i):
         g, s = i // SHOTS, i % SHOTS
@@ -136,6 +138,19 @@
     def rows_of(i):
         return pl.ds(pl.multiple_of(i * W, W), W)
 
+    def p_part(i, side, k):
+        n = i - (CHUNKS - LAST)
+        return pltpu.make_async_remote_copy(
+            src_ref=part.at[n, side, k], dst_ref=home.at[n, side, k],
+            send_sem=part_send.at[side, k, n], recv_sem=part_recv.at[side, k, n],
+            device_id=across[k] if side else peer(HOME[k]), device_id_type=MESH,
+        )
+
+    sides = [(side, k) for side in (0, 1) for k in range(4) if (side, k) != (0, 0)]
+
+    def store(i):
+        return pltpu.make_async_copy(fin.at[:, rows_of(i)], out.at[:, rows_of(i)], sem_out.at[i])
+
     def p_join(i, k):
         return remote(gx.at[i, k], fin.at[mine, rows_of(i)], JOIN + k - 1, i, peer(HOME[k]))
 
@@ -245,24 +260,51 @@
             d6[i, k] = direct(24 + k, d5[i, k], r6[i, k ^ 1])
         p_core(i).start()
 
+    def summed(i, x):
+        there = pl.multiple_of(core * 2 * W + x * W, W)
+        return d6[i, :, pl.ds(there, W)] + rc[i, :, pl.ds(pl.multiple_of(x * W, W), W)]
+
     def stage_core(i):
         p_core(i).wait()
-        away = pl.multiple_of(core * 2 * W + (1 - xlo) * W, W)
-        gx[i] = d6[i, :, pl.ds(away, W)] + rc[i, :, pl.ds(pl.multiple_of((1 - xlo) * W, W), W)]
-        p_xlo(i).start()
+
+        @pl.when(i < CHUNKS - LAST)
+        def _():
+            gx[i] = summed(i, 1 - xlo)
+            p_xlo(i).start()
+
+        @pl.when(i >= CHUNKS - LAST)
+        def _():
+            part[i - (CHUNKS - LAST), 1] = summed(i, 1 - xlo)
+            part[i - (CHUNKS - LAST), 0] = summed(i, xlo)
+            for side, k in sides:
+                p_part(i, side, k).start()
 
     def stage_xlo(i):
-        p_xlo(i).wait()
-        stay = pl.multiple_of(core * 2 * W + xlo * W, W)
-        total = d6[i, :, pl.ds(stay, W)] + rc[i, :, pl.ds(pl.multiple_of(xlo * W, W), W)] + rx[i]
-        fin[mine, rows_of(i)] = total[0]
-        gx[i] = total
-        for k in (1, 2, 3):
-            p_join(i, k).start()
+        @pl.when(i < CHUNKS - LAST)
+        def _():
+            p_xlo(i).wait()
+            total = summed(i, xlo) + rx[i]
+            fin[mine, rows_of(i)] = total[0]
+            gx[i] = total
+            for k in (1, 2, 3):
+                p_join(i, k).start()
 
     def stage_done(i):
-        for k in (1, 2, 3):
-            p_join(i, k).wait()
+        @pl.when(i < CHUNKS - LAST)
+        def _():
+            for k in (1, 2, 3):
+                p_join(i, k).wait()
+
+        @pl.when(i >= CHUNKS - LAST)
+        def _():
+            n = i - (CHUNKS - LAST)
+            for side, k in sides:
+                p_part(i, side, k).wait()
+            fin[mine, rows_of(i)] = part[n, 0, 0] + home[n, 1, 0]
+            for k in (1, 2, 3):
+                fin[flip(mine, k), rows_of(i)] = home[n, 0, k] + home[n, 1, k]
+
+        store(i).start()
 
     start_maps(2)
     start_maps(4)
@@ -308,7 +350,12 @@
         return carry
 
     lax.fori_loop(0, CHUNKS + LAG["done"], tick, 0)
-    out[...] = fin[...]
+
+    def wait_store(i, carry):
+        store(i).wait()
+        return carry
+
+    lax.fori_loop(0, CHUNKS, wait_store, 0)
 
 
 def evaluate_kernel(coef_in, evaluate_in, image, coef, evaluate, part, sem_coef, sem_evaluate, sem_image):
@@ -351,7 +398,7 @@
         kernel,
         out_shape=jax.ShapeDtypeStruct((BOX, rows, K), F32),
         in_specs=[any_space] * 4,
-        out_specs=pl.BlockSpec(memory_space=pltpu.VMEM),
+        out_specs=any_space,
         scratch_shapes=[
             vmem((GROUPS * SHOTS, BOX, Q, 128), F32),
             vmem((BOX, K, Q), F32),
@@ -369,13 +416,18 @@
             vmem((n, 4, 2 * W, K), F32),
             vmem((n, 4, W, K), F32),
             vmem((n, 4, W, K), F32),
+            vmem((LAST, 2, 4, W, K), F32),
+            vmem((LAST, 2, 4, W, K), F32),
             vmem((BOX, rows, K), F32),
             pltpu.SemaphoreType.DMA((GROUPS * SHOTS,)),
+            pltpu.SemaphoreType.DMA((n,)),
             pltpu.SemaphoreType.DMA((3,)),
             pltpu.SemaphoreType.DMA((2, 5, 3)),
             pltpu.SemaphoreType.DMA((2, 5, 3)),
             pltpu.SemaphoreType.DMA((PHASES, n)),
             pltpu.SemaphoreType.DMA((PHASES, n)),
+            pltpu.SemaphoreType.DMA((2, 4, LAST)),
+            pltpu.SemaphoreType.DMA((2, 4, LAST)),
         ],
         compiler_params=pltpu.CompilerParams(
             collective_id=0, has_side_effects=True, vmem_limit_bytes=60 * 2**20
@@ -395,7 +447,7 @@
             pltpu.SemaphoreType.DMA((BOX,)),
             pltpu.SemaphoreType.DMA((BOX,)),
         ],
-        compiler_params=pltpu.CompilerParams(vmem_limit_bytes=32 * 2**20),
+        compiler_params=pltpu.CompilerParams(vmem_limit_bytes=60 * 2**20),
     )(coef, evaluate)
 
 

time: 120 us -> 117 us (0.975)
  Pallas kernels: 119 us -> 117 us
    pallas_call x1, Pallas kernels: 115 us -> 114 us  [shards(): pl.pallas_call(kernel, out_shape=jax.ShapeDtypeStruct((BOX, rows, K), F32...]
where the time goes in v3:
time: 117 us
  Pallas kernels  117 us (100%)
    pallas_call x1, Pallas kernels, shards(): pl.pallas_call(kernel, out_shape=jax.ShapeDtypeStruct((BOX, rows, K), F32...  114 us
    pallas_call x1, Pallas kernels, shards(): pl.pallas_call(evaluate_kernel, out_shape=jax.ShapeDtypeStruct((rows, BOX...  3.54 us

profile of v3, /device:TPU:1, one launch (start us, length us, event | category | flops | bytes accessed | tf_op | source)
XLA Modules:
  0.0 117.3 jit_solution(15695147580158644602)
XLA Ops:
  0.0 113.7 %shard_map.55.coef_in = f32[4,384,128]{2,1,0:T(8,128)} custom-call(f32[1,4,512,1536]{3,2,1,0:T(8,128)} %samples.1, f32[1,4,128,512]{3,2,1,0:T(8,128)} %first.1, f32[7,1,4,128,128]{4,3,2,1,0:T(8,128)} %selfs.1, f32[7,1,4,128,128]{4,3,2,1,0:T(8,128)} %crosses.1), custom_call_target="tpu_custom_call" | custom-call | tf_op jit(solution)/shard_map/pallas_call | solution.py:397
  113.8 3.5 %shard_map.56 = f32[384,2048]{1,0:T(8,128)} custom-call(f32[4,384,128]{2,1,0:T(8,128)} %shard_map.55.coef_in, f32[4,512,128]{2,1,0:T(8,128)} %evaluate_in.1), custom_call_target="tpu_custom_call" | custom-call | tf_op jit(solution)/shard_map/pallas_call | solution.py:437

commit v4 on v3

--- a/solution.py
+++ b/solution.py
@@ -22,8 +22,9 @@
 W = WIDTH // SHOTS
 LAST = 2
 LAG = {"first": 0} | {
-    name: PER_GROUP + lag for name, lag in dict(local=0, z=5, swap=8, y1=12, core=13, xlo=15, done=18).items()
+    name: PER_GROUP + lag for name, lag in dict(local=0, z=2, swap=5, y1=9, core=10, xlo=12, done=15).items()
 }
+EXTRA = (1, 2, 4)
 ORDER = ("local", "xlo", "core", "swap", "z", "done", "y1", "first")
 IN_Z = {1: 1, 2: 2, 3: 3}
 SWAP = {1: 9, 2: 6, 3: 15}
@@ -207,9 +208,13 @@
         if CHUNKS > GROUPS * SHOTS:
             every = CHUNKS // (GROUPS * SHOTS)
 
-            @pl.when(t % every == 0)
+            @pl.when(jnp.logical_and(t < PER_GROUP, t % every == 0))
             def _():
                 first_block(t // every)
+
+            @pl.when(jnp.logical_and(t >= PER_GROUP, t < PER_GROUP + (GROUPS - 1) * SHOTS))
+            def _():
+                first_block(t - PER_GROUP + SHOTS)
         else:
             several = GROUPS * SHOTS // CHUNKS
             for n in range(several):
@@ -230,7 +235,17 @@
 
         lax.fori_loop(0, BOX, one, 0)
 
-    def stage_local(i):
+    def stage_local(t):
+        def ahead(t):
+            return t + sum(jnp.where(t > extra, 1, 0) for extra in EXTRA)
+
+        def one(i, carry):
+            local_chunk(i)
+            return carry
+
+        lax.fori_loop(ahead(t), jnp.minimum(ahead(t + 1), CHUNKS), one, 0)
+
+    def local_chunk(i):
         x = apply(1, apply(0, [c0[i, box] for box in range(BOX)]))
         for box in range(BOX):
             c0[i, box] = x[box]

time: 117 us -> 117 us (level)
  no operation moved by 1% of the time
where the time goes in v4:
time: 117 us
  Pallas kernels  117 us (100%)
    pallas_call x1, Pallas kernels, shards(): pl.pallas_call(kernel, out_shape=jax.ShapeDtypeStruct((BOX, rows, K), F32...  113 us
    pallas_call x1, Pallas kernels, shards(): pl.pallas_call(evaluate_kernel, out_shape=jax.ShapeDtypeStruct((rows, BOX...  3.54 us

profile of v4, /device:TPU:1, one launch (start us, length us, event | category | flops | bytes accessed | tf_op | source)
XLA Modules:
  0.0 116.8 jit_solution(6929206618832825115)
XLA Ops:
  0.0 113.2 %shard_map.55.coef_in = f32[4,384,128]{2,1,0:T(8,128)} custom-call(f32[1,4,512,1536]{3,2,1,0:T(8,128)} %samples.1, f32[1,4,128,512]{3,2,1,0:T(8,128)} %first.1, f32[7,1,4,128,128]{4,3,2,1,0:T(8,128)} %selfs.1, f32[7,1,4,128,128]{4,3,2,1,0:T(8,128)} %crosses.1), custom_call_target="tpu_custom_call" | custom-call | tf_op jit(solution)/shard_map/pallas_call | solution.py:412
  113.2 3.5 %shard_map.56 = f32[384,2048]{1,0:T(8,128)} custom-call(f32[4,384,128]{2,1,0:T(8,128)} %shard_map.55.coef_in, f32[4,512,128]{2,1,0:T(8,128)} %evaluate_in.1), custom_call_target="tpu_custom_call" | custom-call | tf_op jit(solution)/shard_map/pallas_call | solution.py:452
